TPU v7x, 256 devices: a whole 4x4x8 slice. The times are simulated.
256 devices in a mesh: slab: 64 (over y, x_lo, z), head: 4 (over x_hi, core).
Axes of the slice: x: 4 (x_hi: 2, x_lo: 2; x = x_hi * 2 + x_lo), y: 4, z: 8, core: 2. Of those that a mesh axis runs over, the one named last changes fastest.
Arguments:
- query_rows: bfloat16 [65536, 1536], P('slab', 'head'), may hold values from -110 to 110
- key_rows: bfloat16 [65536, 1536], P('slab', 'head'), may hold values from -4 to 4
- value_rows: bfloat16 [65536, 1536], P('slab', 'head'), may hold values from -6 to 6
- far_slab: int32 [128, 48], P('slab'), may hold values from 0 to 63, all different within a row; in each aligned block of 2 rows (0 to 1, 2 to 3, ...) at most 2 rows name the same one
- far_tile: int32 [128, 48], P('slab'), may hold values from 0 to 15
- far_count: int32 [128], P('slab'), may hold values from 24 to 48
- out_weight: bfloat16 [1536, 3072], P('head'), may hold values from -8 to 8
Outputs:
- block_output: bfloat16 [65536, 3072], P('slab', 'head')
Inputs may be any that keep to these rules, and one draw needn't show every extreme that they name: `far_slab`: each row lists 48 different slabs.
All inputs are finite; a program needn't handle non-finite values.
Results may differ from a plain program's by a relative error of at most 0.0057.
Values may be sent and summed in bfloat16 or wider, within the bound.
A program may use at most 128 MiB of HBM per device.

v0:
```python
import math

import jax
import jax.numpy as jnp
from jax import lax
from jax.sharding import PartitionSpec as P

HEAD_DIM = 128
KTILE = 64
NEAR = 256


NEG_BIG = -1e30


def padded(cells, sides, width):
    for axis, dim in sides:
        count = lax.axis_size(axis)
        ends = count - 1
        head = lax.slice_in_dim(cells, 0, width, axis=dim)
        tail = lax.slice_in_dim(cells, cells.shape[dim] - width, cells.shape[dim], axis=dim)
        cells = jnp.concatenate(
            [
                lax.ppermute(tail, axis, [(i, (i + 1) % count) for i in range(ends)]),
                cells,
                lax.ppermute(head, axis, [((i + 1) % count, i) for i in range(ends)]),
            ],
            axis=dim,
        )
    return cells


def attend(query_tile, all_kv, all_ok, heads_dev):
    width = heads_dev * HEAD_DIM
    scale = 1.0 / math.sqrt(HEAD_DIM)
    query_heads = query_tile.reshape(-1, heads_dev, HEAD_DIM).transpose(1, 0, 2)
    key_heads = all_kv[:, :width].reshape(-1, heads_dev, HEAD_DIM).transpose(1, 0, 2)
    value_heads = all_kv[:, width:].reshape(-1, heads_dev, HEAD_DIM).transpose(1, 0, 2)

    def one_head(inputs):
        query_one, key_one, value_one = inputs
        scores = (
            lax.dot_general(
                query_one, key_one, (((1,), (1,)), ((), ())), preferred_element_type=jnp.float32
            )
            * scale
        )
        scores = jnp.where(all_ok[None, :], scores, NEG_BIG)
        highest = jnp.max(scores, axis=1, keepdims=True)
        weights = jnp.exp(scores - highest)
        probs = (weights / jnp.sum(weights, axis=1, keepdims=True)).astype(jnp.bfloat16)
        return jnp.dot(probs, value_one, preferred_element_type=jnp.float32).astype(jnp.bfloat16)

    results = lax.map(one_head, (query_heads, key_heads, value_heads))
    return results.transpose(1, 0, 2).reshape(-1, width)


def body(query_rows, key_rows, value_rows, far_slab, far_tile, far_count, out_weight):
    slab_count = lax.axis_size("slab")
    slab_index = lax.axis_index("slab")
    tok_dev = query_rows.shape[0]
    width = query_rows.shape[1]
    heads_dev = width // HEAD_DIM
    tiles_dev = far_slab.shape[0]
    far_slots = far_slab.shape[1]
    query_tile = tok_dev // tiles_dev
    key_tiles = tok_dev // KTILE
    kv_local = jnp.concatenate([key_rows, value_rows], axis=1)
    widened = padded(kv_local, (("slab", 0),), NEAR)
    position = slab_index * tok_dev - NEAR + jnp.arange(tok_dev + 2 * NEAR, dtype=jnp.int32)
    near_ok = (position >= 0) & (position < slab_count * tok_dev)
    owners = jnp.arange(slab_count, dtype=jnp.int32)
    matches = far_slab[None, :, :] == owners[:, None, None]
    requests = jnp.sum(jnp.where(matches, far_tile[None, :, :], 0), axis=2)
    kv_tiles = kv_local.reshape(key_tiles, KTILE, 2 * width)
    picked = jnp.take(
        kv_tiles, lax.all_to_all(requests, "slab", split_axis=0, concat_axis=0, tiled=True), axis=0
    )
    fetched = lax.all_to_all(picked, "slab", split_axis=0, concat_axis=0, tiled=True)
    slot_index = jnp.arange(far_slots, dtype=jnp.int32)
    results = []
    for tile_index in range(tiles_dev):
        far_kv = fetched[far_slab[tile_index], tile_index].reshape(far_slots * KTILE, 2 * width)
        far_ok = jnp.repeat(slot_index < far_count[tile_index], KTILE)
        all_kv = jnp.concatenate([widened, far_kv], axis=0)
        all_ok = jnp.concatenate([near_ok, far_ok], axis=0)
        queries = query_rows[tile_index * query_tile : (tile_index + 1) * query_tile]
        results.append(attend(queries, all_kv, all_ok, heads_dev))
    attended = jnp.concatenate(results, axis=0)
    all_heads = lax.all_gather(attended, "head", axis=1, tiled=True)
    weight_block = lax.all_to_all(out_weight, "head", split_axis=1, concat_axis=0, tiled=True)
    return jnp.dot(all_heads, weight_block, preferred_element_type=jnp.float32).astype(jnp.bfloat16)


def solution(mesh):
    return jax.shard_map(
        body,
        mesh=mesh,
        in_specs=(
            P("slab", "head"),
            P("slab", "head"),
            P("slab", "head"),
            P("slab", None),
            P("slab", None),
            P("slab"),
            P("head", None),
        ),
        out_specs=P("slab", "head"),
        check_vma=False,
    )
```

profile of v0, /device:TPU:1, one launch (start us, length us, event | category | flops | bytes accessed | tf_op | source)
XLA Modules:
  0.0 526.0 jit_solution(8574328195681579104)
XLA Ops:
  8.1 13.6 %all-to-all-start = ((s32[64,1,2]{2,1,0:T(1,128)}), s32[64,1,2]{2,1,0:T(1,128)S(1)}, u32[]{:S(2)}, u32[]{:S(2)}) async-start(s32[64,1,2]{2,1,0:T(1,128)} %copy.64), calls=%async_computation | async-start | bytes 65536 | tf_op jit(solution)/shard_map/all_to_all | solution.py:77
  24.2 6.7 %all-to-all-done = s32[64,1,2]{2,1,0:T(1,128)S(1)} async-done(((s32[64,1,2]{2,1,0:T(1,128)}), s32[64,1,2]{2,1,0:T(1,128)S(1)}, u32[]{:S(2)}, u32[]{:S(2)}) %all-to-all-start) | async-done | bytes 544 | tf_op jit(solution)/shard_map/all_to_all | solution.py:77
  31.3 8.4 %gather_fusion = bf16[128,64,768]{2,1,0:T(8,128)(2,1)} fusion(bf16[16,64,768]{2,1,0:T(8,128)(2,1)S(1)} %bitcast.110, s32[1024]{0:T(1024)S(1)} %pad_clamp_fusion), kind=kCustom, calls=%fused_computation | custom fusion | bytes 25166336 | tf_op jit(solution)/shard_map/jit(_take)/gather | solution.py:76
  39.6 10.8 %broadcast_select_fusion = bf16[64,2,64,768]{3,2,1,0:T(8,128)(2,1)} fusion(bf16[64,2,64,768]{3,2,1,0:T(8,128)(2,1)} %bitcast.111, pred[64,2]{1,0:T(8,128)(4,1)S(1)} %copy.66), kind=kLoop, calls=%fused_computation.43 | loop fusion | flops 6291456 | bytes 25165952 | tf_op jit(solution)/shard_map/jit(_take)/select_n | solution.py:76
  50.5 5.9 %all-to-all-start.1 = ((bf16[64,2,64,768]{3,2,1,0:T(8,128)(2,1)}), bf16[64,2,64,768]{3,2,1,0:T(8,128)(2,1)}, u32[]{:S(2)}, u32[]{:S(2)}) async-start(bf16[64,2,64,768]{3,2,1,0:T(8,128)(2,1)} %broadcast_select_fusion), calls=%async_computation.1 | async-start | bytes 25165824 | tf_op jit(solution)/shard_map/all_to_all | solution.py:79
  68.0 259.6 %all-to-all-done.1 = bf16[64,2,64,768]{3,2,1,0:T(8,128)(2,1)} async-done(((bf16[64,2,64,768]{3,2,1,0:T(8,128)(2,1)}), bf16[64,2,64,768]{3,2,1,0:T(8,128)(2,1)}, u32[]{:S(2)}, u32[]{:S(2)}) %all-to-all-start.1) | async-done | bytes 12582944 | tf_op jit(solution)/shard_map/all_to_all | solution.py:79
  327.6 7.6 %gather_fusion.1 = bf16[48,64,768]{2,1,0:T(8,128)(2,1)} fusion(bf16[64,2,64,768]{3,2,1,0:T(8,128)(2,1)} %all-to-all-done.1, s32[48]{0:T(128)S(1)} %get-tuple-element.159), kind=kCustom, calls=%fused_computation.1 | custom fusion | bytes 9437568 | tf_op jit(solution)/shard_map/gather | solution.py:83
  335.2 7.7 %gather_fusion.2 = bf16[48,64,768]{2,1,0:T(8,128)(2,1)} fusion(bf16[64,2,64,768]{3,2,1,0:T(8,128)(2,1)} %all-to-all-done.1, s32[48]{0:T(128)S(1)} %get-tuple-element.160), kind=kCustom, calls=%fused_computation.2 | custom fusion | bytes 9437568 | tf_op jit(solution)/shard_map/gather | solution.py:83
  342.9 4.8 pad_maximum_fusion
  347.7 5.2 fusion.50
  352.9 4.3 copy.69
  357.3 5.8 %copy.70 = bf16[4608,384]{0,1:T(8,128)(2,1)} copy(bf16[4608,384]{1,0:T(8,128)(2,1)} %get-tuple-element.147) | data formatting | bytes 7077888 | tf_op jit(solution)/shard_map/slice | solution.py:38
  363.9 36.3 %while.20 = (s32[]{:T(128)}, bf16[3,512,128]{1,2,0:T(8,128)(2,1)}, pred[4608]{0:T(1024)(128)(4,1)S(1)}, bf16[3,512,128]{1,2,0:T(8,128)(2,1)}, bf16[3,4608,128]{1...) while((s32[]{:T(128)}, bf16[3,512,128]{1,2,0:T(8,128)(2,1)}, pred[4608]{0:T(1024)(128)(4,1)S(1)}, ...), condition=%wide.region_4.5_spmd, body=%wide.region_1.0_spmd.sunk | while | flops 1236335616 | bytes 31483980 | solution.py:54
  368.6 4.2 fusion.68
  380.7 4.2 fusion.68
  400.2 4.3 copy.76
  404.5 5.8 %copy.77 = bf16[4608,384]{0,1:T(8,128)(2,1)} copy(bf16[4608,384]{1,0:T(8,128)(2,1)} %get-tuple-element.164) | data formatting | bytes 7077888 | tf_op jit(solution)/shard_map/slice | solution.py:38
  411.1 36.3 %while.21 = (s32[]{:T(128)}, bf16[3,512,128]{1,2,0:T(8,128)(2,1)}, pred[4608]{0:T(1024)(128)(4,1)S(1)}, bf16[3,512,128]{1,2,0:T(8,128)(2,1)}, bf16[3,4608,128]{1...) while((s32[]{:T(128)}, bf16[3,512,128]{1,2,0:T(8,128)(2,1)}, pred[4608]{0:T(1024)(128)(4,1)S(1)}, ...), condition=%wide.region_8.9_spmd, body=%wide.region_5.8_spmd.sunk | while | flops 1236335616 | bytes 31483980 | solution.py:54
  415.8 4.2 fusion.72
  427.9 4.2 fusion.72
  440.0 4.2 fusion.72
  449.4 4.3 copy.82
  453.8 56.3 %all_to_all.39 = bf16[384,4,768]{0,2,1:T(8,128)(2,1)S(1)} all-to-all(bf16[384,4,768]{0,2,1:T(8,128)(2,1)} %bitcast.117), channel_id=1, replica_groups=mesh['slab'=64,'head'=4] {'head'}, dimensions={1} | all-to-all | bytes 4718592 | tf_op jit(solution)/shard_map/all_to_all | solution.py:91
  512.7 6.5 %convolution_convert_fusion = bf16[1024,768]{1,0:T(8,128)(2,1)} fusion(bf16[1024,1536]{0,1:T(8,128)(2,1)} %all-gather.2.cloned.1.call-done, bf16[1536,768]{1,0:T(8,128)(2,1)} %bitcast.122), kind=kOutput, calls=%fused_computation.47 | convolution fusion | flops 2416705536 | bytes 7077888 | tf_op jit(solution)/shard_map/dot_general | solution.py:92
  (67 shorter events, 74.1 us)
Async XLA Ops:
  8.1 22.8 %all-to-all-start = ((s32[64,1,2]{2,1,0:T(1,128)}), s32[64,1,2]{2,1,0:T(1,128)S(1)}, u32[]{:S(2)}, u32[]{:S(2)}) async-start(s32[64,1,2]{2,1,0:T(1,128)} %copy.64), calls=%async_computation | async-start | bytes 65536 | tf_op jit(solution)/shard_map/all_to_all | solution.py:77
  50.5 11.8 %copy-start.2 = (s32[2]{0:T(128)S(1)}, s32[2]{0:T(128)}, u32[]{:S(2)}) copy-start(s32[2]{0:T(128)} %param.16) | copy-start | bytes 28
  50.5 14.2 %copy-start.1 = (bf16[1024,384]{1,0:T(8,128)(2,1)S(1)}, bf16[1024,384]{1,0:T(8,128)(2,1)}, u32[]{:S(2)}) copy-start(bf16[1024,384]{1,0:T(8,128)(2,1)} %param.11) | copy-start | bytes 2359300
  50.5 277.1 %all-to-all-start.1 = ((bf16[64,2,64,768]{3,2,1,0:T(8,128)(2,1)}), bf16[64,2,64,768]{3,2,1,0:T(8,128)(2,1)}, u32[]{:S(2)}, u32[]{:S(2)}) async-start(bf16[64,2,64,768]{3,2,1,0:T(8,128)(2,1)} %broadcast_select_fusion), calls=%async_computation.1 | async-start | bytes 25165824 | tf_op jit(solution)/shard_map/all_to_all | solution.py:79
  56.4 456.3 %all-gather.2.cloned.1.call-start = ((), (), s32[]{:S(2)}) async-start(), calls=%async_computation.3 | async-start | bytes 3932160 | tf_op jit(solution)/shard_map/all_gather | solution.py:90
  57.3 285.6 %collective-permute-start = (bf16[256,768]{1,0:T(8,128)(2,1)}, bf16[256,768]{1,0:T(8,128)(2,1)}, u32[]{:S(2)}, u32[]{:S(2)}) collective-permute-start(bf16[256,768]{1,0:T(8,128)(2,1)} %get-tuple-element.153), channel_id=1, source_target_pairs={{0,4},{4,8},{8,12},{12,16},{16,20},{20,24},{24,28},{28,32},{32,36}... | collective-permute-start | bytes 1179656 | tf_op jit(solution)/shard_map/ppermute | solution.py:24
  60.8 282.1 %collective-permute-start.1 = (bf16[256,768]{1,0:T(8,128)(2,1)S(1)}, bf16[256,768]{1,0:T(8,128)(2,1)}, u32[]{:S(2)}, u32[]{:S(2)}) collective-permute-start(bf16[256,768]{1,0:T(8,128)(2,1)S(1)} %get-tuple-element.154), channel_id=1, source_target_pairs={{4,0},{8,4},{12,8},{16,12},{20,16},{24,20},{28,24},{32,28},{36,32}... | collective-permute-start | bytes 1179656 | tf_op jit(solution)/shard_map/ppermute | solution.py:26
  400.2 10.9 %copy-start = (pred[4608]{0:T(1024)(128)(4,1)S(1)}, pred[4608]{0:T(1024)(128)(4,1)}, u32[]{:S(2)}) copy-start(pred[4608]{0:T(1024)(128)(4,1)} %get-tuple-element.249) | copy-start | bytes 13828
Sparse Core Ops, SparseCore 0:
  449.6 56.7 all-gather.1
where the time goes:
time: 529 us; the launch traced here: 526 us
  waiting for transfers between devices  266 us (50%)
  local copies, waits for them, and re-layouts  84.6 us (16%)
  blocking collectives  56.3 us (11%)
  matrix products  46.8 us (9%)
  other arithmetic  34 us (6%)
  starting transfers between devices  24.5 us (5%)
  between operations  13.5 us (3%)
    all_to_all x1, waiting for transfers between devices, body(): lax.all_to_all(picked, 'slab', split_axis=0, concat_axis=0, tiled=True)  260 us
    all_to_all x1, blocking collectives, body(): lax.all_to_all(out_weight, 'head', split_axis=1, concat_axis=0, tiled=True)  56.3 us
    dot_general x6, matrix products, one_head(): jnp.dot(probs, value_one, preferred_element_type=jnp.float32)  24.9 us
    dynamic_update_slice x12, local copies, waits for them, and re-layouts, attend(): results = lax.map(one_head, (query_heads, key_heads, value_heads))  19.4 us
    slice x3, local copies, waits for them, and re-layouts, attend(): all_kv[:, width:].reshape(-1, heads_dev, HEAD_DIM).transpose(1, 0, 2)  16.8 us
    dot_general x6, matrix products, one_head(): lax.dot_general(query_one, key_one, (((1,), (1,)), ((), ())), preferred_e...  15.4 us
    gather x2, local copies, waits for them, and re-layouts, body(): fetched[far_slab[tile_index], tile_index]  15.3 us
    all_to_all x1, starting transfers between devices, body(): lax.all_to_all(requests, 'slab', split_axis=0, concat_axis=0, tiled=True)  13.6 us
  transfers between devices with their start and end apart: 5, of which 2 were waited for; matrix products, arithmetic and copies ran while one was open for 6% of the time, Pallas kernels for 0%

commit v1 on v0

v1 whole, which is shorter than its diff:
```python
import math

import jax
import jax.numpy as jnp
from jax import lax
from jax.experimental import pallas as pl
from jax.experimental.pallas import tpu as pltpu
from jax.sharding import PartitionSpec as P

HD = 128
KTILE = 64
NEAR = 256
TOK = 1024
KT = TOK // KTILE
NT = NEAR // KTILE
H = 3
NY, NX, NZ = 4, 2, 8
NG = NY * NX
NHEAD = 4
SLABS = NG * NZ
SLOTS = 48
QC = 256
OUTC = 768
NEG = -1e30
SCALE = math.log2(math.e) / math.sqrt(HD)
MESH = pl.DeviceIdType.MESH


def kernel(q_hbm, k_hbm, v_hbm, fs, ft, fc, w_hbm, out_ref, *scratch):
    (own, near, qv, send, recv, att, wr, oacc, mst, lst, acc, bias, nbias, reqv, reqr, reqs,
     zs, zr, ps, pr, rs, rr, hs, hr, ws, wrs, ats, atr, loc) = scratch[:29]
    zrefs = scratch[29:]
    offs = (1, 2, 3, 4, -1, -2, -3)
    zb = {(o, h): zrefs[i * H + h] for i, o in enumerate(offs) for h in range(H)}

    s = lax.axis_index("slab")
    g = lax.axis_index("head")
    z = lax.rem(s, NZ)
    x = lax.rem(lax.div(s, NZ), NX)
    y = lax.div(s, NZ * NX)
    base = s - z

    zright = base + lax.rem(z + 1, NZ)
    zleft = base + lax.rem(z + NZ - 1, NZ)
    snext = lax.rem(s + 1, SLABS)
    sprev = lax.rem(s + SLABS - 1, SLABS)
    xflip = s + NZ * (1 - 2 * x)
    gcore = g + 1 - 2 * lax.rem(g, 2)
    gx = lax.rem(g + 2, NHEAD)
    gxc = gx + 1 - 2 * lax.rem(gx, 2)

    def group_dst(d):
        return (lax.rem(y + lax.div(d, NX), NY) * NX + lax.rem(x + lax.rem(d, NX), NX)) * NZ + z

    def group_src(d):
        return lax.rem(y + NY - lax.div(d, NX), NY) * NX + lax.rem(x + lax.rem(d, NX), NX)

    def remote(src, dst, ssem, rsem, slab, head):
        return pltpu.make_async_remote_copy(
            src_ref=src, dst_ref=dst, send_sem=ssem, recv_sem=rsem,
            device_id=(slab, head), device_id_type=MESH)

    loads = []
    for h in range(H):
        cols = slice(h * HD, (h + 1) * HD)
        loads.append(pltpu.make_async_copy(k_hbm.at[:, :, cols], own.at[h, 0], loc.at[2 * h]))
        loads.append(pltpu.make_async_copy(v_hbm.at[:, :, cols], own.at[h, 1], loc.at[2 * h + 1]))
    for c in loads:
        c.start()
    qload = pltpu.make_async_copy(q_hbm, qv, loc.at[6])
    qload.start()

    barrier = pltpu.get_barrier_semaphore()

    def greet(slab, head):
        pl.semaphore_signal(barrier, inc=1, device_id=(slab, head), device_id_type=MESH)

    for slab, head in ((zright, g), (zleft, g), (snext, g), (sprev, g), (s, gcore), (s, gx),
                       (xflip, gx), (xflip, gxc)):
        greet(slab, head)

    @pl.loop(1, NG)
    def _(d):
        greet(group_dst(d), g)

    for c in loads:
        c.wait()
    pl.semaphore_wait(barrier, 8 + NG - 1)

    zcopies = {}

    def z_start(h, step):
        for kv in range(2):
            for way, sign, target in ((0, -1, zright), (1, 1, zleft)):
                if step == NZ // 2 and way != kv:
                    continue
                src = own.at[h, kv] if step == 1 else zb[sign * (step - 1), h].at[kv]
                dst = zb[NZ // 2 if step == NZ // 2 else sign * step, h].at[kv]
                c = remote(src, dst, zs.at[way, h, step - 1, kv], zr.at[way, h, step - 1, kv], target, g)
                c.start()
                zcopies[way, h, step, kv] = c

    z_start(0, 1)

    lane = lax.broadcasted_iota(jnp.int32, (SLABS, 128), 1)
    row = lax.broadcasted_iota(jnp.int32, (SLABS, 128), 0)

    def want(j, table):
        for r in range(2):
            table = jnp.where((row == fs[r, j]) & (lane == r), ft[r, j], table)
        return table

    reqv[...] = lax.fori_loop(0, SLOTS, want, jnp.zeros((SLABS, 128), jnp.int32))

    def req_copy(d):
        ring = group_src(d)
        return remote(reqv.at[pl.ds(pl.multiple_of(ring * NZ, NZ), NZ)], reqr.at[d], rs.at[d], rr.at[d],
                      ring * NZ + z, g)

    @pl.loop(1, NG)
    def _(d):
        req_copy(d).start()

    reqr[0] = reqv[pl.ds(pl.multiple_of(base, NZ), NZ), :]

    mid = pltpu.make_async_copy(own, near.at[:, :, NT:NT + KT], loc.at[7])
    mid.start()
    halo = [
        remote(own.at[:, :, KT - NT:], near.at[:, :, :NT], hs.at[0], hr.at[0], snext, g),
        remote(own.at[:, :, :NT], near.at[:, :, NT + KT:], hs.at[1], hr.at[1], sprev, g),
    ]
    for c in halo:
        c.start()

    @pl.loop(1, NG)
    def _(d):
        req_copy(d).wait_recv()

    tosm = pltpu.make_async_copy(reqr, reqs, loc.at[8])
    tosm.start()
    tosm.wait()

    def tile_copy(h, step, d):
        b = step % (NZ // 2)
        if b == 0:
            half = 0 if step == 0 else 1
            rows = slice(half * KTILE, (half + 1) * KTILE)
        else:
            rows = slice(0, 2 * KTILE)
        return remote(send.at[h, b, d, :, :, rows, :], recv.at[h, b, d, :, :, rows, :],
                      ps.at[h, step, d], pr.at[h, step, d], group_dst(d), g)

    def select(h, step):
        b = step % (NZ // 2)
        if step == 0:
            parts = ((own, 0, 0),)
        elif b == 0:
            parts = ((zb[NZ // 2, h], NZ // 2, 1),)
        else:
            parts = ((zb[step, h], step, 0), (zb[-step, h], -step, 1))

        def pick(d, dst):
            for ref, off, half in parts:
                zz = lax.rem(z + (off + NZ), NZ)
                for r in range(2):
                    tile = reqs[d, zz, r]
                    for kv in range(2):
                        got = own[h, kv, tile] if step == 0 else ref[kv, tile]
                        dst[h, b, d, kv, r, half * KTILE:(half + 1) * KTILE, :] = got

        @pl.loop(1, NG)
        def _(d):
            pick(d, send)
            tile_copy(h, step, d).start()

        pick(0, recv)

    for h in range(H):
        select(h, 0)

    def w_cols(j):
        return w_hbm.at[:, :, pl.ds(pl.multiple_of(j * OUTC, OUTC), OUTC)]

    w_rows = wr.at[:, pl.ds(pl.multiple_of(g * HD, HD), HD), :]
    wown = pltpu.make_async_copy(w_cols(g), w_rows, loc.at[9])
    wown.start()
    wcopies = [
        remote(w_cols(j), w_rows, ws.at[i], wrs.at[i], slab, j)
        for i, (slab, j) in enumerate(((s, gcore), (xflip, gx), (xflip, gxc)))
    ]
    for c in wcopies:
        c.start()

    key = lax.broadcasted_iota(jnp.int32, (8, NG * 2 * KTILE), 1)
    blk = lax.broadcasted_iota(jnp.int32, (8, NG * 2 * KTILE), 0)
    d_of = key // (2 * KTILE)
    half = (key // KTILE) % 2
    off = jnp.where(blk == 0, half * (NZ // 2), jnp.where(half == 0, blk, NZ - blk))
    ring = ((y + NY - d_of // NX) % NY) * NX + (x + d_of % NX) % NX
    slab_of = ring * NZ + (z + off) % NZ
    for r in range(2):
        count = fc[r]

        def mark(j, table):
            return jnp.where((slab_of == fs[r, j]) & (j < count), 0.0, table)

        bias[r] = lax.fori_loop(0, SLOTS, mark, jnp.full((8, NG * 2 * KTILE), NEG, jnp.float32))
    pos = lax.broadcasted_iota(jnp.int32, (1, TOK + 2 * NEAR), 1) + (s * TOK - NEAR)
    nbias[...] = jnp.where((pos >= 0) & (pos < SLABS * TOK), 0.0, NEG)

    def attend(h, i, keys, values, mask, first):
        rows = pl.ds(pl.multiple_of(i * QC, QC), QC)
        scores = lax.dot_general(qv[rows, h * HD:(h + 1) * HD], keys, (((1,), (1,)), ((), ())),
                                 preferred_element_type=jnp.float32)
        scores = scores * SCALE + mask
        top = jnp.max(scores, axis=1, keepdims=True)
        if not first:
            before = mst[rows, :1]
            top = jnp.maximum(before, top)
        weights = jnp.exp2(scores - top)
        total = jnp.sum(weights, axis=1, keepdims=True)
        mixed = jnp.dot(weights.astype(jnp.bfloat16), values, preferred_element_type=jnp.float32)
        if not first:
            fade = jnp.exp2(before - top)
            total = total + fade * lst[rows, :1]
            mixed = mixed + fade * acc[rows, :]
        return rows, top, total, mixed

    def keep(rows, top, total, mixed):
        mst[rows, :] = jnp.broadcast_to(top, (QC, 128))
        lst[rows, :] = jnp.broadcast_to(total, (QC, 128))
        acc[rows, :] = mixed

    def attend_near(h):
        if h == 0:
            qload.wait()
            mid.wait()
            for c in halo:
                c.wait_recv()

        @pl.loop(0, TOK // QC)
        def _(i):
            keep(*attend(h, i, near[h, 0].reshape(-1, HD), near[h, 1].reshape(-1, HD), nbias[...], True))

    def attend_far(h, b):
        for step in ((0, NZ // 2) if b == 0 else (b,)):
            @pl.loop(1, NG)
            def _(d):
                tile_copy(h, step, d).wait_recv()

        @pl.loop(0, TOK // QC)
        def _(i):
            r = lax.div(i, TOK // 2 // QC)
            keys = recv[h, b, :, 0, r].reshape(NG * 2 * KTILE, HD)
            values = recv[h, b, :, 1, r].reshape(NG * 2 * KTILE, HD)
            got = attend(h, i, keys, values, bias[r, b:b + 1, :], False)
            if b != 0:
                keep(*got)
            else:
                rows, _, total, mixed = got
                att[h, g, rows, :] = (mixed / total).astype(jnp.bfloat16)

    acopies = {}

    def share(h):
        for i, head in ((0, gcore), (1, gx)):
            acopies[h, i] = remote(att.at[h, g], att.at[h, g], ats.at[h, i], atr.at[h, i], s, head)
            acopies[h, i].start()

    def relay(h):
        acopies[h, 1].wait_recv()
        acopies[h, 2] = remote(att.at[h, gx], att.at[h, gx], ats.at[h, 2], atr.at[h, 2], s, gcore)
        acopies[h, 2].start()

    def project(h):
        acopies[h, 0].wait_recv()
        acopies[h, 2].wait_recv()
        if h == 0:
            wown.wait()
            for c in wcopies:
                c.wait_recv()

        @pl.loop(0, TOK // QC)
        def _(i):
            rows = pl.ds(pl.multiple_of(i * QC, QC), QC)
            left = jnp.concatenate([att[h, j, rows, :] for j in range(NHEAD)], axis=1)
            part = jnp.dot(left, wr[h], preferred_element_type=jnp.float32)
            if h > 0:
                part = part + oacc[rows, :]
            if h < H - 1:
                oacc[rows, :] = part
            else:
                out_ref[rows, :] = part.astype(jnp.bfloat16)

    items = []
    for h in range(H):
        for n, b in enumerate((1, 2, 3, 0)):
            def item(h=h, b=b, n=n):
                if n == 0:
                    attend_near(h)
                attend_far(h, b)
                if b == 0:
                    share(h)
                if h > 0 and n == 0:
                    relay(h - 1)
                if h > 0 and n == 1:
                    project(h - 1)
            items.append(item)

    LAG = 4
    done = 0
    stage = 0
    for h in range(H):
        for step in range(1, NZ // 2 + 1):
            for kv in range(2):
                for way in range(2):
                    if (way, h, step, kv) in zcopies:
                        zcopies[way, h, step, kv].wait_recv()
            if step < NZ // 2:
                z_start(h, step + 1)
            if step == NZ // 2 - 1 and h + 1 < H:
                z_start(h + 1, 1)
            select(h, step)
            stage += 1
            if stage > LAG:
                items[done]()
                done += 1
    while done < len(items):
        items[done]()
        done += 1
    relay(H - 1)
    project(H - 1)

    for c in zcopies.values():
        c.wait_send()
    for h in range(H):
        for step in range(NZ // 2 + 1):
            @pl.loop(1, NG)
            def _(d):
                tile_copy(h, step, d).wait_send()

    @pl.loop(1, NG)
    def _(d):
        req_copy(d).wait_send()

    for c in halo + wcopies + list(acopies.values()):
        c.wait_send()


def body(query_rows, key_rows, value_rows, far_slab, far_tile, far_count, out_weight):
    vm = pltpu.VMEM
    dma = pltpu.SemaphoreType.DMA
    bf = jnp.bfloat16
    f32 = jnp.float32
    any_spec = pl.BlockSpec(memory_space=pl.ANY)
    smem_spec = pl.BlockSpec(memory_space=pltpu.SMEM)
    scratch = [
        vm((H, 2, KT, KTILE, HD), bf),
        vm((H, 2, KT + 2 * NT, KTILE, HD), bf),
        vm((TOK, H * HD), bf),
        vm((H, NZ // 2, NG, 2, 2, 2 * KTILE, HD), bf),
        vm((H, NZ // 2, NG, 2, 2, 2 * KTILE, HD), bf),
        vm((H, NHEAD, TOK, HD), bf),
        vm((H, NHEAD * HD, OUTC), bf),
        vm((TOK, OUTC), f32),
        vm((TOK, 128), f32),
        vm((TOK, 128), f32),
        vm((TOK, HD), f32),
        vm((2, 8, NG * 2 * KTILE), f32),
        vm((1, TOK + 2 * NEAR), f32),
        vm((SLABS, 128), jnp.int32),
        vm((NG, NZ, 128), jnp.int32),
        pltpu.SMEM((NG, NZ, 128), jnp.int32),
        dma((2, H, NZ // 2, 2)), dma((2, H, NZ // 2, 2)),
        dma((H, NZ // 2 + 1, NG)), dma((H, NZ // 2 + 1, NG)),
        dma((NG,)), dma((NG,)),
        dma((2,)), dma((2,)),
        dma((3,)), dma((3,)),
        dma((H, 3)), dma((H, 3)),
        dma((10,)),
    ] + [vm((2, KT, KTILE, HD), bf) for _ in range((NZ - 1) * H)]
    call = pl.pallas_call(
        kernel,
        out_shape=jax.ShapeDtypeStruct((TOK, OUTC), bf),
        in_specs=[any_spec, any_spec, any_spec, smem_spec, smem_spec, smem_spec, any_spec],
        out_specs=pl.BlockSpec(memory_space=pltpu.VMEM),
        scratch_shapes=scratch,
        compiler_params=pltpu.CompilerParams(
            collective_id=0, has_side_effects=True, vmem_limit_bytes=60 * 1024 * 1024),
        cost_estimate=pl.CostEstimate(
            flops=12_000_000_000, bytes_accessed=8_000_000, transcendentals=18_000_000),
    )
    return call(query_rows, key_rows.reshape(KT, KTILE, H * HD), value_rows.reshape(KT, KTILE, H * HD), far_slab, far_tile, far_count,
                out_weight.reshape(H, HD, NHEAD * OUTC))


def solution(mesh):
    return jax.shard_map(
        body,
        mesh=mesh,
        in_specs=(
            P("slab", "head"),
            P("slab", "head"),
            P("slab", "head"),
            P("slab", None),
            P("slab", None),
            P("slab"),
            P("head", None),
        ),
        out_specs=P("slab", "head"),
        check_vma=False,
    )
```

time: 529 us -> 200 us (0.38)
  waiting for transfers between devices: 266 us -> 0 us
  Pallas kernels: 0 us -> 198 us
  local copies, waits for them, and re-layouts: 84.6 us -> 2.65 us
  blocking collectives: 56.3 us -> 0 us
  matrix products: 46.8 us -> 0 us
  other arithmetic: 34 us -> 0 us
  starting transfers between devices: 24.5 us -> 0 us
  between operations: 13.5 us -> 0.01 us
    all_to_all x2 -> x0, waiting for transfers between devices: 266 us -> none  [the longest x1 260 us: body(): lax.all_to_all(picked, 'slab', split_axis=0, concat_axis=0, tiled=True)]
    pallas_call x0 -> x1, Pallas kernels: none -> 198 us  [body(): call(query_rows, key_rows.reshape(KT, KTILE, H * HD), value_rows.reshape(...]
    all_to_all x1 -> x0, blocking collectives: 56.3 us -> none  [body(): lax.all_to_all(out_weight, 'head', split_axis=1, concat_axis=0, tiled=True)]
    dot_general x13 -> x0, matrix products: 46.8 us -> none  [the longest x6 24.9 us: one_head(): jnp.dot(probs, value_one, preferred_element_type=jnp.float32)]
    slice x8 -> x0, local copies, waits for them, and re-layouts: 27.1 us -> none  [the longest x3 16.8 us: attend(): all_kv[:, width:].reshape(-1, heads_dev, HEAD_DIM).transpose(1, 0, 2)]
    gather x3 -> x0, local copies, waits for them, and re-layouts: 23.7 us -> none  [the longest x2 15.3 us: body(): fetched[far_slab[tile_index], tile_index]]
    all_to_all x2 -> x0, starting transfers between devices: 19.5 us -> none  [the longest x1 13.6 us: body(): lax.all_to_all(requests, 'slab', split_axis=0, concat_axis=0, tiled=True)]
    dynamic_update_slice x12 -> x0, local copies, waits for them, and re-layouts: 19.4 us -> none  [attend(): results = lax.map(one_head, (query_heads, key_heads, value_heads))]
  transfers between devices with their start and end apart: 5 -> 0, of which waited for: 2 -> 0; matrix products, arithmetic and copies ran while one was open for 6% -> 0% of each run, Pallas kernels for 0% -> 0%
where the time goes in v1:
time: 200 us
  Pallas kernels  198 us (99%)
  local copies, waits for them, and re-layouts  2.65 us (1%)
    pallas_call x1, Pallas kernels, body(): call(query_rows, key_rows.reshape(KT, KTILE, H * HD), value_rows.reshape(...  198 us

profile of v1, /device:TPU:1, one launch (start us, length us, event | category | flops | bytes accessed | tf_op | source)
XLA Modules:
  0.0 200.3 jit_solution(9267040393101877626)
XLA Ops:
  0.0 197.6 %shard_map.73 = bf16[1024,768]{1,0:T(8,128)(2,1)} custom-call(bf16[1024,384]{1,0:T(8,128)(2,1)} %q_hbm.1, bf16[16,64,384]{2,1,0:T(8,128)(2,1)} %bitcast.4, bf16[16,64,384]{2,1,0:T(8,128)(2,1)} %bitcast.5, s32[2,48]{1,0:T(2,128)} %fs.1, s32[2,48]{1,0:T(2,128)} %ft.1, s32[2]{0:T(128)} %fc.1, bf16[3,128,3072]{2,1,0:T(8,128)(2,1)} %bitcast.3), custom_call_target="tpu_custom_call" | custom-call | flops 12000000000 | bytes 8000000 | tf_op jit(solution)/shard_map/pallas_call | solution.py:393
  197.6 2.7 %copy.9 = bf16[1024,768]{1,0:T(8,128)(2,1)} copy(bf16[1024,768]{1,0:T(8,128)(2,1)} %shard_map.73) | data formatting | bytes 3145728

commit v2 on v1

v2 whole, which is shorter than its diff:
```python
import math

import jax
import jax.numpy as jnp
from jax import lax
from jax.experimental import pallas as pl
from jax.experimental.pallas import tpu as pltpu
from jax.sharding import PartitionSpec as P

HD = 128
KTILE = 64
NEAR = 256
TOK = 1024
KT = TOK // KTILE
NT = NEAR // KTILE
H = 3
NY, NX, NZ = 4, 2, 8
NG = NY * NX
NHEAD = 4
SLABS = NG * NZ
SLOTS = 48
QC = 256
OUTC = 768
HX, KX = -1, 0
NEG = -1e30
SCALE = math.log2(math.e) / math.sqrt(HD)
MESH = pl.DeviceIdType.MESH
HALF = TOK // 2
STAGES = ((0, 1), (0, 2), (1, 1), (0, 3), (1, 2), (0, 4), (1, 3), (2, 1), (1, 4), (2, 2), (2, 3), (2, 4))
STARTS = (((0, 1), 1), ((0, 3), 2))
LAG = 5
BETWEEN = {(2, 2): ((0, 0),), (2, 3): ((1, 0), (0, 1)), (2, 4): ((1, 1),)}


def kernel(q_hbm, k_hbm, v_hbm, fs, ft, fc, fsv, ftv, w_hbm, out_ref, *scratch):
    (own, near, qv, send, recv, att, wr, oacc, mst, lst, acc, bias, nbias, pk, pkr, reqv, reqs,
     zs, zr, ps, pr, rs, rr, hs, hr, ws, wrs, ats, atr, xs, loc) = scratch[:31]
    zrefs = scratch[31:]
    offs = (1, 2, 3, 4, -1, -2, -3)
    zb = {(o, h): zrefs[i * H + h] for i, o in enumerate(offs) for h in range(H)}
    xrefs = zrefs[len(offs) * H:]
    xb = {o: xrefs[i] for i, o in enumerate((0,) + offs)}

    s = lax.axis_index("slab")
    g = lax.axis_index("head")
    z = lax.rem(s, NZ)
    x = lax.rem(lax.div(s, NZ), NX)
    y = lax.div(s, NZ * NX)
    base = s - z

    zright = base + lax.rem(z + 1, NZ)
    zleft = base + lax.rem(z + NZ - 1, NZ)
    ring_next = lax.rem(s + NZ, SLABS)
    ring_prev = lax.rem(s + SLABS - NZ, SLABS)
    xflip = s + NZ * (1 - 2 * x)
    gcore = g + 1 - 2 * lax.rem(g, 2)
    gx = lax.rem(g + 2, NHEAD)
    gxc = gx + 1 - 2 * lax.rem(gx, 2)

    def group_dst(d):
        return (lax.rem(y + lax.rem(d, NY), NY) * NX + lax.rem(x + lax.div(d, NY), NX)) * NZ + z

    def group_src(d):
        return lax.rem(y + NY - lax.rem(d, NY), NY) * NX + lax.rem(x + lax.div(d, NY), NX)

    def remote(src, dst, ssem, rsem, slab, head):
        return pltpu.make_async_remote_copy(
            src_ref=src, dst_ref=dst, send_sem=ssem, recv_sem=rsem,
            device_id=(slab, head), device_id_type=MESH)

    loads = []
    for h in range(H):
        cols = slice(h * HD, (h + 1) * HD)
        loads.append(pltpu.make_async_copy(k_hbm.at[:, :, cols], own.at[h, 0], loc.at[2 * h]))
        loads.append(pltpu.make_async_copy(v_hbm.at[:, :, cols], own.at[h, 1], loc.at[2 * h + 1]))
    for c in loads:
        c.start()
    qload = pltpu.make_async_copy(q_hbm, qv, loc.at[6])
    qload.start()

    barrier = pltpu.get_barrier_semaphore()

    def greet(slab, head):
        pl.semaphore_signal(barrier, inc=1, device_id=(slab, head), device_id_type=MESH)

    for slab, head in ((zright, g), (zleft, g), (s, gcore), (s, gx),
                       (xflip, gx), (xflip, gxc)):
        greet(slab, head)

    @pl.loop(1, NG)
    def _(d):
        greet(group_dst(d), g)

    for c in loads:
        c.wait()
    pl.semaphore_wait(barrier, 6 + NG - 1)

    zcopies = {}

    def z_start(h, step):
        for c in range(2 if h == HX else 1):
            def at(off):
                if c == 1:
                    return xb[off]
                return own.at[h] if off == 0 else zb[off, h]

            for way, sign, target in ((0, -1, zright), (1, 1, zleft)):
                src = at(sign * (step - 1))
                dst = at(NZ // 2 if step == NZ // 2 else sign * step)
                if step == NZ // 2:
                    part = slice(way * KT // 2, (way + 1) * KT // 2)
                    part = (part,) if c == 1 else (slice(0, 2), part)
                    src, dst = src.at[part], dst.at[part]
                sem = (way, h, step - 1, c)
                zcopies[sem] = remote(src, dst, zs.at[sem], zr.at[sem], target, g)
                zcopies[sem].start()

    z_start(0, 1)

    pk[...] = jnp.full((2, 8, 128), -1, jnp.int32)
    pk[0, :2, :SLOTS] = fsv[...]
    pk[1, :2, :SLOTS] = ftv[...]

    def req_copy(d):
        return remote(pk, pkr.at[d], rs.at[0], rr.at[0], group_src(d) * NZ + z, g)

    req_all = remote(pkr.at[1:], pkr.at[1:], rs.at[0], rr.at[0], s, gcore)

    @pl.loop(1, NG)
    def _(d):
        req_copy(d).start()

    pkr[0] = pk[...]

    mid = pltpu.make_async_copy(own, near.at[:, :, NT:NT + KT], loc.at[7])
    mid.start()

    def halo_up(h):
        return remote(zb[-1, h].at[:, KT - NT:], near.at[h, :, :NT], hs.at[h], hr.at[h], ring_next, g)

    def halo_down(h):
        return remote(zb[1, h].at[:, :NT], near.at[h, :, NT + KT:], hs.at[h], hr.at[h], ring_prev, g)

    def halo_start(h):
        @pl.when(z == 0)
        def _():
            halo_up(h).start()

        @pl.when(z != 0)
        def _():
            near[h, :, :NT] = zb[-1, h][:, KT - NT:]

        @pl.when(z == NZ - 1)
        def _():
            halo_down(h).start()

        @pl.when(z != NZ - 1)
        def _():
            near[h, :, NT + KT:] = zb[1, h][:, :NT]

    def halo_wait(h, sent):
        for end, copy in ((0, halo_up), (NZ - 1, halo_down)):
            @pl.when(z == end)
            def _():
                (copy(h).wait_send if sent else copy(h).wait_recv)()

    req_all.wait_recv()

    listed = pkr[:, 0]
    tiles = pkr[:, 1]
    lane = lax.broadcasted_iota(jnp.int32, (NG, 8, 128), 2)
    table = jnp.zeros((NG, 8, 128), jnp.int32)
    for n in range(2 * NZ):
        first = base if n < NZ else xflip - z
        hit = jnp.where(listed == first + n % NZ, tiles, 0)
        table = jnp.where(lane == n, jnp.sum(hit, axis=2, keepdims=True), table)
    reqv[...] = table
    tosm = pltpu.make_async_copy(reqv, reqs, loc.at[8])
    tosm.start()
    tosm.wait()

    both = slice(0, 2)
    if_plain = ((1, NG, 0, 0, both),)
    if_first = (
        (NY, NG, 0, 0, slice(1 - KX, 2 - KX)),
        (1, NY, 0, 0, both),
        (NY + 1, NG, NY, 1, slice(KX, KX + 1)),
    )

    def groups(h):
        return enumerate(if_first if h == HX else if_plain)

    def tile_refs(h, step, slot, kvs):
        b = step % (NZ // 2)
        rows = slice(0, 2 * KTILE)
        if b == 0:
            half = 0 if step == 0 else 1
            rows = slice(half * KTILE, (half + 1) * KTILE)
        return send.at[h, b, slot, kvs, :, rows, :], recv.at[h, b, slot, kvs, :, rows, :]

    def tile_copy(h, step, n, slot, d, kvs):
        return remote(*tile_refs(h, step, slot, kvs), ps.at[h, step, n], pr.at[h, step, n], group_dst(d), g)

    def tile_all(h, step):
        return [remote(*tile_refs(h, step, slice(lo, hi), kvs), ps.at[h, step, n], pr.at[h, step, n], s, gcore)
                for n, (lo, hi, _, _, kvs) in groups(h)]

    def pick(h, step, slot, d, other, kvs, dst):
        b = step % (NZ // 2)
        for half, off in ((0, 0),) if step == 0 else (((1, step),) if b == 0 else ((0, step), (1, -step))):
            lane_of = lax.rem(z + (off + NZ), NZ) + NZ * other
            for r in range(2):
                tile = reqs[d, r, lane_of]
                for kv in range(kvs.start, kvs.stop):
                    if other:
                        got = xb[off][tile]
                    else:
                        got = own[h, kv, tile] if off == 0 else zb[off, h][kv, tile]
                    dst[h, b, slot, kv, r, half * KTILE:(half + 1) * KTILE, :] = got

    def select(h, step):
        for n, (lo, hi, back, other, kvs) in groups(h):
            @pl.loop(lo, hi)
            def _(slot):
                pick(h, step, slot, slot - back, other, kvs, send)
                tile_copy(h, step, n, slot, slot - back, kvs).start()

        pick(h, step, 0, 0, 0, both, recv)
        if h == HX:
            pick(h, step, NY, 0, 1, slice(KX, KX + 1), recv)

    for h in range(H):
        select(h, 0)

    def w_cols(j):
        return w_hbm.at[:, :, pl.ds(pl.multiple_of(j * OUTC, OUTC), OUTC)]

    w_rows = wr.at[:, pl.ds(pl.multiple_of(g * HD, HD), HD), :]
    wown = pltpu.make_async_copy(w_cols(g), w_rows, loc.at[9])
    wown.start()
    wcopies = [
        remote(w_cols(j), w_rows, ws.at[i], wrs.at[i], slab, j)
        for i, (slab, j) in enumerate(((s, gcore), (xflip, gx), (xflip, gxc)))
    ]
    for c in wcopies:
        c.start()

    key = lax.broadcasted_iota(jnp.int32, (8, NG * 2 * KTILE), 1)
    blk = lax.broadcasted_iota(jnp.int32, (8, NG * 2 * KTILE), 0)
    d_of = jnp.where(blk == 0, (key // KTILE) % NG, key // (2 * KTILE))
    half = jnp.where(blk == 0, key // (NG * KTILE), (key // KTILE) % 2)
    off = jnp.where(blk == 0, half * (NZ // 2), jnp.where(half == 0, blk, NZ - blk))
    ring = ((y + NY - d_of % NY) % NY) * NX + (x + d_of // NY) % NX
    slab_of = ring * NZ + (z + off) % NZ
    for r in range(2):
        count = fc[r]

        def mark(j, table):
            return jnp.where((slab_of == fs[r, j]) & (j < count), 0.0, table)

        bias[r] = lax.fori_loop(0, SLOTS, mark, jnp.full((8, NG * 2 * KTILE), NEG, jnp.float32))
    pos = lax.broadcasted_iota(jnp.int32, (1, TOK + 2 * NEAR), 1) + (s * TOK - NEAR)
    nbias[...] = jnp.where((pos >= 0) & (pos < SLABS * TOK), 0.0, NEG)

    def attend(h, i, keys, values, mask, first):
        rows = pl.ds(pl.multiple_of(i * QC, QC), QC)
        scores = lax.dot_general(qv[rows, h * HD:(h + 1) * HD], keys, (((1,), (1,)), ((), ())),
                                 preferred_element_type=jnp.float32)
        scores = scores * SCALE + mask
        top = jnp.max(scores, axis=1, keepdims=True)
        if not first:
            before = mst[rows, :1]
            top = jnp.maximum(before, top)
        weights = jnp.exp2(scores - top)
        total = jnp.sum(weights, axis=1, keepdims=True)
        mixed = jnp.dot(weights.astype(jnp.bfloat16), values, preferred_element_type=jnp.float32)
        if not first:
            fade = jnp.exp2(before - top)
            total = total + fade * lst[rows, :1]
            mixed = mixed + fade * acc[rows, :]
        return rows, top, total, mixed

    def keep(rows, top, total, mixed):
        mst[rows, :] = jnp.broadcast_to(top, (QC, 128))
        lst[rows, :] = jnp.broadcast_to(total, (QC, 128))
        acc[rows, :] = mixed

    def attend_near(h):
        if h == 0:
            qload.wait()
            mid.wait()
        halo_wait(h, False)

        @pl.loop(0, TOK // QC)
        def _(i):
            keep(*attend(h, i, near[h, 0].reshape(-1, HD), near[h, 1].reshape(-1, HD), nbias[...], True))

    def attend_far(h, step):
        b = step % (NZ // 2)
        for c in tile_all(h, step):
            c.wait_recv()
        half = 0 if step == 0 else 1
        rows = slice(0, 2 * KTILE) if b != 0 else slice(half * KTILE, (half + 1) * KTILE)
        lanes = slice(0, NG * 2 * KTILE) if b != 0 else slice(half * NG * KTILE, (half + 1) * NG * KTILE)

        for part in range(2):
            @pl.loop(part * HALF // QC, (part + 1) * HALF // QC)
            def _(i):
                keys = recv[h, b, :, 0, part, rows].reshape(-1, HD)
                values = recv[h, b, :, 1, part, rows].reshape(-1, HD)
                got = attend(h, i, keys, values, bias[part, b:b + 1, lanes], False)
                if step != NZ // 2:
                    keep(*got)
                else:
                    rows_of, _, total, mixed = got
                    att[h, g, rows_of, :] = (mixed / total).astype(jnp.bfloat16)

            if step == NZ // 2:
                share(h, part)

    acopies = {}

    def att_copy(h, part, i, which, head):
        ref = att.at[h, which, part * HALF:(part + 1) * HALF]
        acopies[h, part, i] = remote(ref, ref, ats.at[h, part, i], atr.at[h, part, i], s, head)
        acopies[h, part, i].start()

    def share(h, part):
        att_copy(h, part, 1, g, gx)
        att_copy(h, part, 0, g, gcore)

    def relay(h, part):
        acopies[h, part, 1].wait_recv()
        att_copy(h, part, 2, gx, gcore)

    def project(h, part):
        acopies[h, part, 0].wait_recv()
        acopies[h, part, 2].wait_recv()
        if h == 0 and part == 0:
            wown.wait()
            for c in wcopies:
                c.wait_recv()

        @pl.loop(part * HALF // QC, (part + 1) * HALF // QC)
        def _(i):
            rows = pl.ds(pl.multiple_of(i * QC, QC), QC)
            left = jnp.concatenate([att[h, j, rows, :] for j in range(NHEAD)], axis=1)
            piece = jnp.dot(left, wr[h], preferred_element_type=jnp.float32)
            if h > 0:
                piece = piece + oacc[rows, :]
            if h < H - 1:
                oacc[rows, :] = piece
            else:
                out_ref[rows, :] = piece.astype(jnp.bfloat16)

    items = []
    for h in range(H):
        for step in range(1, NZ // 2 + 1):
            def item(h=h, step=step):
                for what, of in BETWEEN.get((h, step), ()):
                    for part in range(2):
                        (relay if what == 0 else project)(of, part)
                if step == 1:
                    attend_near(h)
                    attend_far(h, 0)
                attend_far(h, step)
            items.append(item)

    done = 0
    for n, (h, step) in enumerate(STAGES):
        for sem, c in zcopies.items():
            if sem[1:3] == (h, step - 1):
                c.wait_recv()
        if step == 1:
            halo_start(h)
        if step < NZ // 2:
            z_start(h, step + 1)
        for then, what in STARTS:
            if then == (h, step):
                z_start(what, 1)
        select(h, step)
        if n >= LAG:
            items[done]()
            done += 1
    while done < len(items):
        items[done]()
        done += 1
    for part in range(2):
        relay(H - 1, part)
    for part in range(2):
        project(H - 1, part)

    for c in zcopies.values():
        c.wait_send()
    for h in range(H):
        for step in range(NZ // 2 + 1):
            for c in tile_all(h, step):
                c.wait_send()
        halo_wait(h, True)

    req_all.wait_send()

    for c in wcopies + list(acopies.values()):
        c.wait_send()


def body(query_rows, key_rows, value_rows, far_slab, far_tile, far_count, out_weight):
    vm = pltpu.VMEM
    dma = pltpu.SemaphoreType.DMA
    bf = jnp.bfloat16
    f32 = jnp.float32
    any_spec = pl.BlockSpec(memory_space=pl.ANY)
    smem_spec = pl.BlockSpec(memory_space=pltpu.SMEM)
    scratch = [
        vm((H, 2, KT, KTILE, HD), bf),
        vm((H, 2, KT + 2 * NT, KTILE, HD), bf),
        vm((TOK, H * HD), bf),
        vm((H, NZ // 2, NG, 2, 2, 2 * KTILE, HD), bf),
        vm((H, NZ // 2, NG, 2, 2, 2 * KTILE, HD), bf),
        vm((H, NHEAD, TOK, HD), bf),
        vm((H, NHEAD * HD, OUTC), bf),
        vm((TOK, OUTC), f32),
        vm((TOK, 128), f32),
        vm((TOK, 128), f32),
        vm((TOK, HD), f32),
        vm((2, 8, NG * 2 * KTILE), f32),
        vm((1, TOK + 2 * NEAR), f32),
        vm((2, 8, 128), jnp.int32),
        vm((NG, 2, 8, 128), jnp.int32),
        vm((NG, 8, 128), jnp.int32),
        pltpu.SMEM((NG, 8, 128), jnp.int32),
        dma((2, H, NZ // 2, 2)), dma((2, H, NZ // 2, 2)),
        dma((H, NZ // 2 + 1, 3)), dma((H, NZ // 2 + 1, 3)),
        dma((1,)), dma((1,)),
        dma((H,)), dma((H,)),
        dma((3,)), dma((3,)),
        dma((H, 2, 3)), dma((H, 2, 3)),
        dma((2,)),
        dma((10,)),
    ] + [vm((2, KT, KTILE, HD), bf) for _ in range((NZ - 1) * H)]
    scratch += [vm((KT, KTILE, HD), bf) for _ in range(NZ)]
    vmem_spec = pl.BlockSpec(memory_space=pltpu.VMEM)
    call = pl.pallas_call(
        kernel,
        out_shape=jax.ShapeDtypeStruct((TOK, OUTC), bf),
        in_specs=[any_spec, any_spec, any_spec, smem_spec, smem_spec, smem_spec, vmem_spec, vmem_spec, any_spec],
        out_specs=vmem_spec,
        scratch_shapes=scratch,
        compiler_params=pltpu.CompilerParams(
            collective_id=0, has_side_effects=True, vmem_limit_bytes=60 * 1024 * 1024),
        cost_estimate=pl.CostEstimate(
            flops=12_000_000_000, bytes_accessed=8_000_000, transcendentals=18_000_000),
    )
    return call(query_rows, key_rows.reshape(KT, KTILE, H * HD), value_rows.reshape(KT, KTILE, H * HD), far_slab, far_tile, far_count,
                far_slab, far_tile,
                out_weight.reshape(H, HD, NHEAD * OUTC))


def solution(mesh):
    return jax.shard_map(
        body,
        mesh=mesh,
        in_specs=(
            P("slab", "head"),
            P("slab", "head"),
            P("slab", "head"),
            P("slab", None),
            P("slab", None),
            P("slab"),
            P("head", None),
        ),
        out_specs=P("slab", "head"),
        check_vma=False,
    )
```

time: 200 us -> 192 us (0.960)
  Pallas kernels: 198 us -> 189 us
    pallas_call x1, Pallas kernels: 198 us -> 189 us  [body(): call(query_rows, key_rows.reshape(KT, KTILE, H * HD), value_rows.reshape(...]
where the time goes in v2:
time: 192 us
  Pallas kernels  189 us (98%)
  local copies, waits for them, and re-layouts  2.65 us (1%)
    pallas_call x1, Pallas kernels, body(): call(query_rows, key_rows.reshape(KT, KTILE, H * HD), value_rows.reshape(...  189 us

profile of v2, /device:TPU:1, one launch (start us, length us, event | category | flops | bytes accessed | tf_op | source)
XLA Modules:
  0.0 191.8 jit_solution(12212122447625511286)
XLA Ops:
  0.0 189.1 %shard_map.73 = bf16[1024,768]{1,0:T(8,128)(2,1)} custom-call(bf16[1024,384]{1,0:T(8,128)(2,1)} %q_hbm.1, bf16[16,64,384]{2,1,0:T(8,128)(2,1)} %bitcast.4, bf16[16,64,384]{2,1,0:T(8,128)(2,1)} %bitcast.5, s32[2,48]{1,0:T(2,128)} %fsv.1, s32[2,48]{1,0:T(2,128)} %ftv.1, s32[2]{0:T(128)} %fc.1, s32[2,48]{1,0:T(2,128)} %fsv.1, s32[2,48]{1,0:T(2,128)} %ftv.1, ...), custom_call_target="tpu_custom_call" | custom-call | flops 12000000000 | bytes 8000000 | tf_op jit(solution)/shard_map/pallas_call | solution.py:454
  189.1 2.7 %copy.9 = bf16[1024,768]{1,0:T(8,128)(2,1)} copy(bf16[1024,768]{1,0:T(8,128)(2,1)} %shard_map.73) | data formatting | bytes 3145728

commit v3 on v2

--- a/solution.py
+++ b/solution.py
@@ -21,14 +21,15 @@
 SLOTS = 48
 QC = 256
 OUTC = 768
-HX, KX = -1, 0
+HX, KX = 2, 0
 NEG = -1e30
 SCALE = math.log2(math.e) / math.sqrt(HD)
 MESH = pl.DeviceIdType.MESH
 HALF = TOK // 2
-STAGES = ((0, 1), (0, 2), (1, 1), (0, 3), (1, 2), (0, 4), (1, 3), (2, 1), (1, 4), (2, 2), (2, 3), (2, 4))
-STARTS = (((0, 1), 1), ((0, 3), 2))
-LAG = 5
+STAGES = ((0, 1), (0, 2), (1, 1), (0, 3), (1, 2), (0, 4), (1, 3), (2, 1), (1, 4), (2, 2), (3, 1), (2, 3), (3, 2),
+          (2, 4), (3, 3), (3, 4))
+STARTS = (((0, 1), 1), ((0, 3), 2), ((1, 4), 3))
+LAG = 6
 BETWEEN = {(2, 2): ((0, 0),), (2, 3): ((1, 0), (0, 1)), (2, 4): ((1, 1),)}
 
 
@@ -98,24 +99,25 @@
     zcopies = {}
 
     def z_start(h, step):
-        for c in range(2 if h == HX else 1):
-            def at(off):
-                if c == 1:
-                    return xb[off]
-                return own.at[h] if off == 0 else zb[off, h]
-
-            for way, sign, target in ((0, -1, zright), (1, 1, zleft)):
-                src = at(sign * (step - 1))
-                dst = at(NZ // 2 if step == NZ // 2 else sign * step)
-                if step == NZ // 2:
-                    part = slice(way * KT // 2, (way + 1) * KT // 2)
-                    part = (part,) if c == 1 else (slice(0, 2), part)
-                    src, dst = src.at[part], dst.at[part]
-                sem = (way, h, step - 1, c)
-                zcopies[sem] = remote(src, dst, zs.at[sem], zr.at[sem], target, g)
-                zcopies[sem].start()
+        def at(off):
+            if h == H:
+                return xb[off]
+            return own.at[h] if off == 0 else zb[off, h]
+
+        for way, sign, target in ((0, -1, zright), (1, 1, zleft)):
+            src = at(sign * (step - 1))
+            dst = at(NZ // 2 if step == NZ // 2 else sign * step)
+            if step == NZ // 2:
+                part = slice(way * KT // 2, (way + 1) * KT // 2)
+                part = (part,) if h == H else (slice(0, 2), part)
+                src, dst = src.at[part], dst.at[part]
+            sem = (way, h, step - 1)
+            zcopies[sem] = remote(src, dst, zs.at[sem], zr.at[sem], target, g)
+            zcopies[sem].start()
 
     z_start(0, 1)
+    xcopy = remote(own.at[HX, KX], xb[0], xs.at[0], xs.at[1], xflip, g)
+    xcopy.start()
 
     pk[...] = jnp.full((2, 8, 128), -1, jnp.int32)
     pk[0, :2, :SLOTS] = fsv[...]
@@ -219,18 +221,25 @@
                     dst[h, b, slot, kv, r, half * KTILE:(half + 1) * KTILE, :] = got
 
     def select(h, step):
-        for n, (lo, hi, back, other, kvs) in groups(h):
+        here = HX if h == H else h
+        for n, (lo, hi, back, other, kvs) in groups(here):
+            if other != (h == H):
+                continue
+
             @pl.loop(lo, hi)
             def _(slot):
-                pick(h, step, slot, slot - back, other, kvs, send)
-                tile_copy(h, step, n, slot, slot - back, kvs).start()
-
-        pick(h, step, 0, 0, 0, both, recv)
-        if h == HX:
-            pick(h, step, NY, 0, 1, slice(KX, KX + 1), recv)
+                pick(here, step, slot, slot - back, other, kvs, send)
+                tile_copy(here, step, n, slot, slot - back, kvs).start()
+
+        if h == H:
+            pick(HX, step, NY, 0, 1, slice(KX, KX + 1), recv)
+        else:
+            pick(h, step, 0, 0, 0, both, recv)
 
     for h in range(H):
         select(h, 0)
+    xcopy.wait_recv()
+    select(H, 0)
 
     def w_cols(j):
         return w_hbm.at[:, :, pl.ds(pl.multiple_of(j * OUTC, OUTC), OUTC)]
@@ -371,7 +380,7 @@
         for sem, c in zcopies.items():
             if sem[1:3] == (h, step - 1):
                 c.wait_recv()
-        if step == 1:
+        if step == 1 and h < H:
             halo_start(h)
         if step < NZ // 2:
             z_start(h, step + 1)
@@ -390,6 +399,7 @@
     for part in range(2):
         project(H - 1, part)
 
+    xcopy.wait_send()
     for c in zcopies.values():
         c.wait_send()
     for h in range(H):
@@ -429,7 +439,7 @@
         vm((NG, 2, 8, 128), jnp.int32),
         vm((NG, 8, 128), jnp.int32),
         pltpu.SMEM((NG, 8, 128), jnp.int32),
-        dma((2, H, NZ // 2, 2)), dma((2, H, NZ // 2, 2)),
+        dma((2, H + 1, NZ // 2)), dma((2, H + 1, NZ // 2)),
         dma((H, NZ // 2 + 1, 3)), dma((H, NZ // 2 + 1, 3)),
         dma((1,)), dma((1,)),
         dma((H,)), dma((H,)),

time: 192 us -> 189 us (0.984)
  Pallas kernels: 189 us -> 187 us
    pallas_call x1, Pallas kernels: 189 us -> 187 us  [body(): call(query_rows, key_rows.reshape(KT, KTILE, H * HD), value_rows.reshape(...]
where the time goes in v3:
time: 189 us
  Pallas kernels  187 us (99%)
  local copies, waits for them, and re-layouts  2.65 us (1%)
    pallas_call x1, Pallas kernels, body(): call(query_rows, key_rows.reshape(KT, KTILE, H * HD), value_rows.reshape(...  187 us

profile of v3, /device:TPU:1, one launch (start us, length us, event | category | flops | bytes accessed | tf_op | source)
XLA Modules:
  0.0 189.2 jit_solution(7672210662716204788)
XLA Ops:
  0.0 186.6 %shard_map.73 = bf16[1024,768]{1,0:T(8,128)(2,1)} custom-call(bf16[1024,384]{1,0:T(8,128)(2,1)} %q_hbm.1, bf16[16,64,384]{2,1,0:T(8,128)(2,1)} %bitcast.4, bf16[16,64,384]{2,1,0:T(8,128)(2,1)} %bitcast.5, s32[2,48]{1,0:T(2,128)} %fsv.1, s32[2,48]{1,0:T(2,128)} %ftv.1, s32[2]{0:T(128)} %fc.1, s32[2,48]{1,0:T(2,128)} %fsv.1, s32[2,48]{1,0:T(2,128)} %ftv.1, ...), custom_call_target="tpu_custom_call" | custom-call | flops 12000000000 | bytes 8000000 | tf_op jit(solution)/shard_map/pallas_call | solution.py:464
  186.6 2.7 %copy.9 = bf16[1024,768]{1,0:T(8,128)(2,1)} copy(bf16[1024,768]{1,0:T(8,128)(2,1)} %shard_map.73) | data formatting | bytes 3145728

commit v4 on v3

--- a/solution.py
+++ b/solution.py
@@ -30,6 +30,7 @@
           (2, 4), (3, 3), (3, 4))
 STARTS = (((0, 1), 1), ((0, 3), 2), ((1, 4), 3))
 LAG = 6
+NEAR_AT = (4, 8, 11)
 BETWEEN = {(2, 2): ((0, 0),), (2, 3): ((1, 0), (0, 1)), (2, 4): ((1, 1),)}
 
 
@@ -278,21 +279,21 @@
         scores = scores * SCALE + mask
         top = jnp.max(scores, axis=1, keepdims=True)
         if not first:
-            before = mst[rows, :1]
+            before = mst[h, rows, :1]
             top = jnp.maximum(before, top)
         weights = jnp.exp2(scores - top)
         total = jnp.sum(weights, axis=1, keepdims=True)
         mixed = jnp.dot(weights.astype(jnp.bfloat16), values, preferred_element_type=jnp.float32)
         if not first:
             fade = jnp.exp2(before - top)
-            total = total + fade * lst[rows, :1]
-            mixed = mixed + fade * acc[rows, :]
+            total = total + fade * lst[h, rows, :1]
+            mixed = mixed + fade * acc[h, rows, :]
         return rows, top, total, mixed
 
-    def keep(rows, top, total, mixed):
-        mst[rows, :] = jnp.broadcast_to(top, (QC, 128))
-        lst[rows, :] = jnp.broadcast_to(total, (QC, 128))
-        acc[rows, :] = mixed
+    def keep(h, rows, top, total, mixed):
+        mst[h, rows, :] = jnp.broadcast_to(top, (QC, 128))
+        lst[h, rows, :] = jnp.broadcast_to(total, (QC, 128))
+        acc[h, rows, :] = mixed
 
     def attend_near(h):
         if h == 0:
@@ -302,7 +303,7 @@
 
         @pl.loop(0, TOK // QC)
         def _(i):
-            keep(*attend(h, i, near[h, 0].reshape(-1, HD), near[h, 1].reshape(-1, HD), nbias[...], True))
+            keep(h, *attend(h, i, near[h, 0].reshape(-1, HD), near[h, 1].reshape(-1, HD), nbias[...], True))
 
     def attend_far(h, step):
         b = step % (NZ // 2)
@@ -319,7 +320,7 @@
                 values = recv[h, b, :, 1, part, rows].reshape(-1, HD)
                 got = attend(h, i, keys, values, bias[part, b:b + 1, lanes], False)
                 if step != NZ // 2:
-                    keep(*got)
+                    keep(h, *got)
                 else:
                     rows_of, _, total, mixed = got
                     att[h, g, rows_of, :] = (mixed / total).astype(jnp.bfloat16)
@@ -369,9 +370,6 @@
                 for what, of in BETWEEN.get((h, step), ()):
                     for part in range(2):
                         (relay if what == 0 else project)(of, part)
-                if step == 1:
-                    attend_near(h)
-                    attend_far(h, 0)
                 attend_far(h, step)
             items.append(item)
 
@@ -388,6 +386,10 @@
             if then == (h, step):
                 z_start(what, 1)
         select(h, step)
+        for h_near, at_stage in enumerate(NEAR_AT):
+            if n == at_stage:
+                attend_near(h_near)
+                attend_far(h_near, 0)
         if n >= LAG:
             items[done]()
             done += 1
@@ -430,9 +432,9 @@
         vm((H, NHEAD, TOK, HD), bf),
         vm((H, NHEAD * HD, OUTC), bf),
         vm((TOK, OUTC), f32),
-        vm((TOK, 128), f32),
-        vm((TOK, 128), f32),
-        vm((TOK, HD), f32),
+        vm((H, TOK, 128), f32),
+        vm((H, TOK, 128), f32),
+        vm((H, TOK, HD), f32),
         vm((2, 8, NG * 2 * KTILE), f32),
         vm((1, TOK + 2 * NEAR), f32),
         vm((2, 8, 128), jnp.int32),

time: 189 us -> 184 us (0.974)
  Pallas kernels: 187 us -> 182 us
    pallas_call x1, Pallas kernels: 187 us -> 182 us  [body(): call(query_rows, key_rows.reshape(KT, KTILE, H * HD), value_rows.reshape(...]
where the time goes in v4:
time: 184 us
  Pallas kernels  182 us (99%)
  local copies, waits for them, and re-layouts  2.65 us (1%)
    pallas_call x1, Pallas kernels, body(): call(query_rows, key_rows.reshape(KT, KTILE, H * HD), value_rows.reshape(...  182 us

profile of v4, /device:TPU:1, one launch (start us, length us, event | category | flops | bytes accessed | tf_op | source)
XLA Modules:
  0.0 184.3 jit_solution(14721986122018636404)
XLA Ops:
  0.0 181.6 %shard_map.73 = bf16[1024,768]{1,0:T(8,128)(2,1)} custom-call(bf16[1024,384]{1,0:T(8,128)(2,1)} %q_hbm.1, bf16[16,64,384]{2,1,0:T(8,128)(2,1)} %bitcast.4, bf16[16,64,384]{2,1,0:T(8,128)(2,1)} %bitcast.5, s32[2,48]{1,0:T(2,128)} %fsv.1, s32[2,48]{1,0:T(2,128)} %ftv.1, s32[2]{0:T(128)} %fc.1, s32[2,48]{1,0:T(2,128)} %fsv.1, s32[2,48]{1,0:T(2,128)} %ftv.1, ...), custom_call_target="tpu_custom_call" | custom-call | flops 12000000000 | bytes 8000000 | tf_op jit(solution)/shard_map/pallas_call | solution.py:466
  181.6 2.7 %copy.9 = bf16[1024,768]{1,0:T(8,128)(2,1)} copy(bf16[1024,768]{1,0:T(8,128)(2,1)} %shard_map.73) | data formatting | bytes 3145728
